TPU v7x, 256 devices: a whole 4x4x8 slice. The times are simulated.
256 devices in a mesh: job: 32 (over x, y, core), seq: 8 (over z).
Axes of the slice: x: 4, y: 4, z: 8, core: 2. Of those that a mesh axis runs over, the one named last changes fastest.
Arguments:
- text_cache: bfloat16 [32, 2, 512, 4096], P('job', None, 'seq'), may hold values from -6 to 6
- source: int32 [32], replicated, may hold values from 0 to 63, as said below
- text_len: int32 [32], replicated, may hold values from 1 to 512, as said below
- query: bfloat16 [32, 2048, 3072], P('job', 'seq'), may hold values from -64 to 64
- w_text: bfloat16 [4096, 5120], P('job', 'seq'), may hold values from -0.09375 to 0.09375
- b_text: bfloat16 [5120], P('seq'), may hold values from -3 to 3
- w_key: bfloat16 [5120, 3072], P('job', 'seq'), may hold values from -0.078125 to 0.078125
- w_value: bfloat16 [5120, 3072], P('job', 'seq'), may hold values from -0.078125 to 0.078125
- b_value: bfloat16 [3072], P('seq'), may hold values from -3 to 3
Outputs:
- attended: bfloat16 [32, 2048, 3072], P('job', 'seq')
Inputs may be any that keep to these rules, and one draw needn't show every extreme that they name: `source`: entries are distinct flat cache indices; 0 and 63 occur in every draw. `text_len`: some group has 512 live text tokens and some has 1.
All inputs are finite; a program needn't handle non-finite values.
Results may differ from a plain program's by a relative error of at most 0.008.
Values may be sent and summed in bfloat16 or wider, within the bound.
A program may use at most 128 MiB of HBM per device.

v0:
```python
import jax
import jax.numpy as jnp
from jax import lax
from jax.sharding import PartitionSpec as P

HD = 128


def attend(queries, keys, values, key_live):
    score_scale = HD ** (-0.5)
    scores = (
        jnp.einsum("rhd,khd->hrk", queries, keys, preferred_element_type=jnp.float32) * score_scale
    )
    scores = jnp.where(key_live[None, None, :], scores, jnp.float32(-1e30))
    row_peak = jnp.max(scores, axis=-1, keepdims=True)
    exponent = jnp.exp(scores - row_peak)
    probabilities = (exponent / jnp.sum(exponent, axis=-1, keepdims=True)).astype(jnp.bfloat16)
    mixed = jnp.einsum("hrk,khd->rhd", probabilities, values, preferred_element_type=jnp.float32)
    return mixed.astype(jnp.bfloat16).reshape(queries.shape[0], -1)


def add_product(left, portion):
    return jnp.dot(left, portion, preferred_element_type=jnp.float32)


def body(text_cache, source, text_len, query, w_text, b_text, w_key, w_value, b_value):
    groups = lax.axis_size("job")
    group_index = lax.axis_index("job")
    cached = text_cache[0]
    slot_count, rows_local, text_width = cached.shape
    portion_rows = rows_local // groups
    spread = lax.all_to_all(
        cached.reshape(slot_count, groups, portion_rows, text_width),
        "job",
        split_axis=1,
        concat_axis=1,
        tiled=True,
    )
    holder = source // slot_count
    slot_of = source % slot_count
    picked = spread[slot_of, holder]
    arrived = lax.all_to_all(picked, "job", split_axis=0, concat_axis=0, tiled=True).reshape(
        rows_local, text_width
    )
    text_rows = lax.all_gather(arrived, "seq", axis=0, tiled=True)
    text_count = text_rows.shape[0]
    preact = add_product(text_rows, lax.all_gather(w_text, "job", axis=0, tiled=True))
    hidden_part = jax.nn.gelu(preact + b_text.astype(jnp.float32), approximate=True).astype(
        jnp.bfloat16
    )
    hidden = lax.all_gather(hidden_part, "seq", axis=1, tiled=True)

    def single_step(portion):
        return add_product(hidden, portion)

    key_sums = single_step(lax.all_gather(w_key, "job", axis=0, tiled=True))
    value_sums = single_step(lax.all_gather(w_value, "job", axis=0, tiled=True))
    keys = key_sums.astype(jnp.bfloat16)
    values = (value_sums + b_value.astype(jnp.float32)).astype(jnp.bfloat16)
    key_live = jnp.arange(text_count) < text_len[group_index]
    queries = query[0]
    video_local = queries.shape[0]
    all_keys, all_values = (
        lax.all_gather(keys, "seq", axis=1, tiled=True),
        lax.all_gather(values, "seq", axis=1, tiled=True),
    )
    result = attend(
        queries.reshape(video_local, -1, HD),
        all_keys.reshape(text_count, -1, HD),
        all_values.reshape(text_count, -1, HD),
        key_live,
    )
    return result[None]


def solution(mesh):
    in_specs = (
        P("job", None, "seq", None),
        P(),
        P(),
        P("job", "seq", None),
        P("job", "seq"),
        P("seq"),
        P("job", "seq"),
        P("job", "seq"),
        P("seq"),
    )
    out_specs = P("job", "seq", None)
    return jax.shard_map(body, mesh=mesh, in_specs=in_specs, out_specs=out_specs, check_vma=False)
```

profile of v0, /device:TPU:2, one launch (start us, length us, event | category | flops | bytes accessed | tf_op | source)
XLA Modules:
  0.0 443.3 jit_solution(1020585032217924011)
XLA Ops:
  6.5 2.3 copy.20
  8.9 2.1 copy.21
  10.9 7.6 %all-to-all-start = ((bf16[2,32,2,4096]{3,2,0,1:T(2,128)(2,1)}), bf16[2,32,2,4096]{3,2,0,1:T(2,128)(2,1)S(1)}, u32[]{:S(2)}, u32[]{:S(2)}) async-start(bf16[2,32,2,4096]{3,2,0,1:T(2,128)(2,1)} %copy.21), calls=%async_computation | async-start | bytes 2097152 | tf_op jit(solution)/shard_map/all_to_all | solution.py:32
  18.6 0.0 all-gather.8.cloned.1.call-start
  18.7 14.4 %all-to-all-done = bf16[2,32,2,4096]{3,2,0,1:T(2,128)(2,1)S(1)} async-done(((bf16[2,32,2,4096]{3,2,0,1:T(2,128)(2,1)}), bf16[2,32,2,4096]{3,2,0,1:T(2,128)(2,1)S(1)}, u32[]{:S(2)}, u32[]{:S(2)}) %all-to-all-start) | async-done | bytes 1048608 | tf_op jit(solution)/shard_map/all_to_all | solution.py:32
  33.0 1.6 gather_fusion
  34.6 15.9 %all_to_all.10 = bf16[32,2,4096]{2,1,0:T(2,128)(2,1)S(1)} all-to-all(bf16[32,2,4096]{2,1,0:T(2,128)(2,1)S(1)} %gather_fusion), channel_id=1, replica_groups=mesh['job'=32,'seq'=8] {'job'}, dimensions={0} | all-to-all | bytes 1048576 | tf_op jit(solution)/shard_map/all_to_all | solution.py:42
  50.6 1.0 reshape.17
  51.6 0.0 all-gather.10.cloned.1.call-start
  51.6 0.7 all-gather.10.cloned.1.call-update
  52.4 0.7 all-gather.18.cloned.1.call-update
  53.1 54.3 %all-gather.8.cloned.1.call-done = bf16[512,4096]{1,0:T(8,128)(2,1)} async-done(((bf16[64,4096]{1,0:T(8,128)(2,1)}), bf16[512,4096]{1,0:T(8,128)(2,1)}) %all-gather.8.cloned.1.call-update) | async-done | bytes 4194320 | tf_op jit(solution)/shard_map/all_gather | solution.py:45
  107.4 53.3 %all-gather.10.cloned.1.call-done = bf16[4096,640]{1,0:T(8,128)(2,1)} async-done(((bf16[128,640]{1,0:T(8,128)(2,1)}), bf16[4096,640]{1,0:T(8,128)(2,1)}) %all-gather.10.cloned.1.call-update) | async-done | bytes 5242896 | tf_op jit(solution)/shard_map/all_gather | solution.py:47
  160.7 8.2 %fusion.21 = bf16[512,640]{1,0:T(8,128)(2,1)} fusion(bf16[512,4096]{1,0:T(8,128)(2,1)} %all-gather.8.cloned.1.call-done, bf16[4096,640]{1,0:T(8,128)(2,1)} %all-gather.10.cloned.1.call-done, f32[640]{0:T(1024)S(1)} %convert_element_type.24), kind=kOutput, calls=%fused_computation.26 | convolution fusion | flops 2687631360 | bytes 10095104 | tf_op jit(solution)/shard_map/dot_general | solution.py:23
  169.0 0.0 all-gather.14.cloned.1.call-start
  169.0 0.5 all-gather.14.cloned.1.call-update
  169.6 43.9 %all-gather.18.cloned.1.call-done = bf16[5120,384]{1,0:T(8,128)(2,1)} async-done(((bf16[160,384]{1,0:T(8,128)(2,1)}), bf16[5120,384]{1,0:T(8,128)(2,1)}) %all-gather.18.cloned.1.call-update) | async-done | bytes 3932176 | tf_op jit(solution)/shard_map/all_gather | solution.py:56
  213.5 66.1 %all-gather.12.cloned.1.call-done = bf16[512,5120]{1,0:T(8,128)(2,1)} async-done(((bf16[512,640]{1,0:T(8,128)(2,1)}), bf16[512,5120]{1,0:T(8,128)(2,1)}) %all-gather.12.cloned.1.call-update) | async-done | bytes 5242896 | tf_op jit(solution)/shard_map/all_gather | solution.py:51
  279.6 7.3 %convolution_convert_fusion = bf16[512,384]{1,0:T(8,128)(2,1)} fusion(bf16[512,5120]{1,0:T(8,128)(2,1)} %all-gather.12.cloned.1.call-done, bf16[5120,384]{1,0:T(8,128)(2,1)} %all-gather.18.cloned.1.call-done), kind=kOutput, calls=%fused_computation.29 | convolution fusion | flops 2013462528 | bytes 9568256 | tf_op jit(solution)/shard_map/dot_general | solution.py:23
  286.9 0.2 all-gather.16.cloned.1.call-start
  287.2 43.9 %all-gather.14.cloned.1.call-done = bf16[5120,384]{1,0:T(8,128)(2,1)} async-done(((bf16[160,384]{1,0:T(8,128)(2,1)}), bf16[5120,384]{1,0:T(8,128)(2,1)}) %all-gather.14.cloned.1.call-update) | async-done | bytes 3932176 | tf_op jit(solution)/shard_map/all_gather | solution.py:57
  331.1 7.3 %fusion.22 = bf16[512,384]{1,0:T(8,128)(2,1)} fusion(bf16[512,5120]{1,0:T(8,128)(2,1)} %all-gather.12.cloned.1.call-done, bf16[5120,384]{1,0:T(8,128)(2,1)} %all-gather.14.cloned.1.call-done, f32[384]{0:T(512)S(1)} %convert_element_type.26), kind=kOutput, calls=%fused_computation.28 | convolution fusion | flops 2013659136 | bytes 9569792 | tf_op jit(solution)/shard_map/dot_general | solution.py:23
  338.5 0.3 copy.30
  338.8 0.6 dynamic_slice.3
  339.4 0.6 iota_compare_fusion
  340.0 38.0 %all-gather.20.cloned.1.call-done = bf16[512,3072]{1,0:T(8,128)(2,1)} async-done(((bf16[512,384]{1,0:T(8,128)(2,1)}), bf16[512,3072]{1,0:T(8,128)(2,1)}) %all-gather.20.cloned.1.call-update) | async-done | bytes 3145744 | tf_op jit(solution)/shard_map/all_gather | solution.py:64
  378.0 3.7 fusion.9
  381.7 9.1 %fusion.30 = (f32[24,256]{1,0:T(8,128)S(1)}, f32[24,256,512]{1,2,0:T(8,128)}) fusion(f32[24,512,256]{2,1,0:T(8,128)S(1)} %fusion.9, pred[512]{0:T(512)(128)(4,1)S(1)} %iota_compare_fusion), kind=kOutput, calls=%fused_computation.45 | output fusion | flops 18874880 | bytes 25190912 | tf_op jit(solution)/shard_map/sub | solution.py:16
  390.7 33.1 %all-gather.16.cloned.1.call-done = bf16[512,3072]{1,0:T(8,128)(2,1)} async-done(((bf16[512,384]{1,0:T(8,128)(2,1)}), bf16[512,3072]{1,0:T(8,128)(2,1)}) %all-gather.16.cloned.1.call-update) | async-done | bytes 3145744 | tf_op jit(solution)/shard_map/all_gather | solution.py:65
  423.9 3.2 copy.28
  427.1 6.8 %fusion.12 = bf16[24,128,256]{2,1,0:T(8,128)(2,1)} fusion(bf16[512,24,128]{0,2,1:T(8,128)(2,1)S(1)} %bitcast.36, f32[24,256,512]{1,2,0:T(8,128)} %get-tuple-element.6, f32[24,256]{1,0:T(8,128)S(1)} %get-tuple-element.5), kind=kOutput, calls=%fused_computation.16 | convolution fusion | flops 812384256 | bytes 17326080 | tf_op jit(solution)/shard_map/hrk,khd->rhd/dot_general | solution.py:18
  433.9 2.6 copy.26
  (20 shorter events, 0.2 us)
Async XLA Ops:
  6.5 12.1 %copy-start.3 = (s32[32]{0:T(128)S(1)}, s32[32]{0:T(128)}, u32[]{:S(2)}) copy-start(s32[32]{0:T(128)} %param.10) | copy-start | bytes 388
  8.9 44.2 %copy-start.1 = (bf16[640]{0:T(1024)(128)(2,1)S(1)}, bf16[640]{0:T(1024)(128)(2,1)}, u32[]{:S(2)}) copy-start(bf16[640]{0:T(1024)(128)(2,1)} %param.14) | copy-start | bytes 3844
  10.9 22.1 %all-to-all-start = ((bf16[2,32,2,4096]{3,2,0,1:T(2,128)(2,1)}), bf16[2,32,2,4096]{3,2,0,1:T(2,128)(2,1)S(1)}, u32[]{:S(2)}, u32[]{:S(2)}) async-start(bf16[2,32,2,4096]{3,2,0,1:T(2,128)(2,1)} %copy.21), calls=%async_computation | async-start | bytes 2097152 | tf_op jit(solution)/shard_map/all_to_all | solution.py:32
  18.6 88.9 %all-gather.8.cloned.1.call-start = ((), (), s32[]{:S(2)}) async-start(), calls=%async_computation.2 | async-start | bytes 4718592 | tf_op jit(solution)/shard_map/all_gather | solution.py:45
  51.6 109.1 %all-gather.10.cloned.1.call-start = ((), (), s32[]{:S(2)}) async-start(), calls=%async_computation.3 | async-start | bytes 5406720 | tf_op jit(solution)/shard_map/all_gather | solution.py:47
  52.3 161.2 %all-gather.18.cloned.1.call-start = ((), (), s32[]{:S(2)}) async-start(), calls=%async_computation.7 | async-start | bytes 4055040 | tf_op jit(solution)/shard_map/all_gather | solution.py:56
  53.1 226.6 %all-gather.12.cloned.1.call-start = ((), (), s32[]{:S(2)}) async-start(), calls=%async_computation.4 | async-start | bytes 5898240 | tf_op jit(solution)/shard_map/all_gather | solution.py:51
  169.0 162.1 %all-gather.14.cloned.1.call-start = ((), (), s32[]{:S(2)}) async-start(), calls=%async_computation.5 | async-start | bytes 4055040 | tf_op jit(solution)/shard_map/all_gather | solution.py:57
  169.6 117.6 %copy-start.2 = (bf16[384]{0:T(512)(128)(2,1)S(1)}, bf16[384]{0:T(512)(128)(2,1)}, u32[]{:S(2)}) copy-start(bf16[384]{0:T(512)(128)(2,1)} %param.17) | copy-start | bytes 2308
  169.6 208.4 %all-gather.20.cloned.1.call-start = ((), (), s32[]{:S(2)}) async-start(), calls=%async_computation.8 | async-start | bytes 3538944 | tf_op jit(solution)/shard_map/all_gather | solution.py:64
  286.9 136.9 %all-gather.16.cloned.1.call-start = ((), (), s32[]{:S(2)}) async-start(), calls=%async_computation.6 | async-start | bytes 3538944 | tf_op jit(solution)/shard_map/all_gather | solution.py:65
  287.2 51.3 %copy-start = (bf16[1,256,3072]{2,1,0:T(8,128)(2,1)S(1)}, bf16[1,256,3072]{2,1,0:T(8,128)(2,1)}, u32[]{:S(2)}) copy-start(bf16[1,256,3072]{2,1,0:T(8,128)(2,1)} %param.12) | copy-start | bytes 4718596
  287.2 51.6 %copy-start.4 = (s32[32]{0:T(128)S(1)}, s32[32]{0:T(128)}, u32[]{:S(2)}) copy-start(s32[32]{0:T(128)} %param.11) | copy-start | bytes 388
Sparse Core Ops, SparseCore 0:
  51.7 55.6 all-gather.7
  110.0 50.7 all-gather.9
  163.3 50.2 all-gather.17
  215.2 64.3 all-gather.11
  282.0 49.0 all-gather.13
  332.7 45.2 all-gather.19
  379.8 44.0 all-gather.15
where the time goes:
time: 444 us; the launch traced here: 443 us
  waiting for transfers between devices  349 us (79%)
  matrix products  33.4 us (8%)
  blocking collectives  15.9 us (4%)
  local copies, waits for them, and re-layouts  13.7 us (3%)
  between operations  13.6 us (3%)
  other arithmetic  9.71 us (2%)
  starting transfers between devices  8.08 us (2%)
    all_gather x1, waiting for transfers between devices, body(): hidden = lax.all_gather(hidden_part, 'seq', axis=1, tiled=True)  66.1 us
    all_gather x1, waiting for transfers between devices, body(): text_rows = lax.all_gather(arrived, 'seq', axis=0, tiled=True)  54.3 us
    all_gather x1, waiting for transfers between devices, body(): lax.all_gather(w_text, 'job', axis=0, tiled=True)  53.3 us
    all_gather x1, waiting for transfers between devices, body(): key_sums = single_step(lax.all_gather(w_key, 'job', axis=0, tiled=True))  43.9 us
    all_gather x1, waiting for transfers between devices, body(): value_sums = single_step(lax.all_gather(w_value, 'job', axis=0, tiled=True))  43.9 us
    all_gather x1, waiting for transfers between devices, body(): lax.all_gather(keys, 'seq', axis=1, tiled=True)  38 us
    all_gather x1, waiting for transfers between devices, body(): lax.all_gather(values, 'seq', axis=1, tiled=True)  33.1 us
    dot_general x3, matrix products, add_product(): return jnp.dot(left, portion, preferred_element_type=jnp.float32)  22.9 us
  transfers between devices with their start and end apart: 8, of which 8 were waited for; matrix products, arithmetic and copies ran while one was open for 8% of the time, Pallas kernels for 0%

commit v1 on v0

--- a/solution.py
+++ b/solution.py
@@ -48,7 +48,9 @@
     hidden_part = jax.nn.gelu(preact + b_text.astype(jnp.float32), approximate=True).astype(
         jnp.bfloat16
     )
-    hidden = lax.all_gather(hidden_part, "seq", axis=1, tiled=True)
+    hidden = jnp.concatenate(
+        lax.all_to_all(jnp.stack([hidden_part] * lax.axis_size("seq")), "seq", 0, 0), axis=1
+    )
 
     def single_step(portion):
         return add_product(hidden, portion)

time: 444 us -> 411 us (0.926)
  waiting for transfers between devices: 349 us -> 307 us
  starting transfers between devices: 8.08 us -> 15.1 us
    all_to_all x0 -> x1, waiting for transfers between devices: none -> 84 us  [body(): lax.all_to_all(jnp.stack([hidden_part] * lax.axis_size('seq')), 'seq', 0, 0)]
    all_gather x1 -> x0, waiting for transfers between devices: 66.1 us -> none  [body(): hidden = lax.all_gather(hidden_part, 'seq', axis=1, tiled=True)]
    all_gather x1, waiting for transfers between devices: 43.9 us -> 0.02 us  [body(): value_sums = single_step(lax.all_gather(w_value, 'job', axis=0, tiled=True))]
    all_gather x1, waiting for transfers between devices: 43.9 us -> 34.7 us  [body(): key_sums = single_step(lax.all_gather(w_key, 'job', axis=0, tiled=True))]
    all_gather x1, waiting for transfers between devices: 38 us -> 30.9 us  [body(): lax.all_gather(keys, 'seq', axis=1, tiled=True)]
    all_to_all x0 -> x1, starting transfers between devices: none -> 7.01 us  [body(): lax.all_to_all(jnp.stack([hidden_part] * lax.axis_size('seq')), 'seq', 0, 0)]
  transfers between devices with their start and end apart: 8 -> 8, of which waited for: 8 -> 7; matrix products, arithmetic and copies ran while one was open for 8% -> 10% of each run, Pallas kernels for 0% -> 0%
where the time goes in v1:
time: 411 us; the launch traced here: 410 us
  waiting for transfers between devices  307 us (75%)
  matrix products  32.7 us (8%)
  local copies, waits for them, and re-layouts  16.8 us (4%)
  blocking collectives  15.9 us (4%)
  starting transfers between devices  15.1 us (4%)
  between operations  13.6 us (3%)
  other arithmetic  9.7 us (2%)
    all_to_all x1, waiting for transfers between devices, body(): lax.all_to_all(jnp.stack([hidden_part] * lax.axis_size('seq')), 'seq', 0, 0)  84 us
    all_gather x1, waiting for transfers between devices, body(): text_rows = lax.all_gather(arrived, 'seq', axis=0, tiled=True)  54.3 us
    all_gather x1, waiting for transfers between devices, body(): lax.all_gather(w_text, 'job', axis=0, tiled=True)  53.3 us
    all_gather x1, waiting for transfers between devices, body(): key_sums = single_step(lax.all_gather(w_key, 'job', axis=0, tiled=True))  34.7 us
    all_gather x1, waiting for transfers between devices, body(): lax.all_gather(values, 'seq', axis=1, tiled=True)  33 us
    all_gather x1, waiting for transfers between devices, body(): lax.all_gather(keys, 'seq', axis=1, tiled=True)  30.9 us
    dot_general x3, matrix products, add_product(): return jnp.dot(left, portion, preferred_element_type=jnp.float32)  22.2 us
    all_to_all x1, blocking collectives, body(): lax.all_to_all(picked, 'job', split_axis=0, concat_axis=0, tiled=True)  15.9 us
  transfers between devices with their start and end apart: 8, of which 7 were waited for; matrix products, arithmetic and copies ran while one was open for 10% of the time, Pallas kernels for 0%

profile of v1, /device:TPU:2, one launch (start us, length us, event | category | flops | bytes accessed | tf_op | source)
XLA Modules:
  0.0 410.4 jit_solution(2933499488446111123)
XLA Ops:
  6.5 2.3 copy.27
  8.9 2.1 copy.28
  10.9 7.6 %all-to-all-start = ((bf16[2,32,2,4096]{3,2,0,1:T(2,128)(2,1)}), bf16[2,32,2,4096]{3,2,0,1:T(2,128)(2,1)S(1)}, u32[]{:S(2)}, u32[]{:S(2)}) async-start(bf16[2,32,2,4096]{3,2,0,1:T(2,128)(2,1)} %copy.28), calls=%async_computation | async-start | bytes 2097152 | tf_op jit(solution)/shard_map/all_to_all | solution.py:32
  18.7 14.4 %all-to-all-done = bf16[2,32,2,4096]{3,2,0,1:T(2,128)(2,1)S(1)} async-done(((bf16[2,32,2,4096]{3,2,0,1:T(2,128)(2,1)}), bf16[2,32,2,4096]{3,2,0,1:T(2,128)(2,1)S(1)}, u32[]{:S(2)}, u32[]{:S(2)}) %all-to-all-start) | async-done | bytes 1048608 | tf_op jit(solution)/shard_map/all_to_all | solution.py:32
  33.0 1.6 gather_fusion
  34.6 15.9 %all_to_all.15 = bf16[32,2,4096]{2,1,0:T(2,128)(2,1)S(1)} all-to-all(bf16[32,2,4096]{2,1,0:T(2,128)(2,1)S(1)} %gather_fusion), channel_id=1, replica_groups=mesh['job'=32,'seq'=8] {'job'}, dimensions={0} | all-to-all | bytes 1048576 | tf_op jit(solution)/shard_map/all_to_all | solution.py:42
  50.6 1.0 reshape.25
  51.6 0.0 all-gather.9.cloned.1.call-start
  51.6 0.7 all-gather.9.cloned.1.call-update
  52.4 0.7 all-gather.15.cloned.1.call-update
  53.1 54.3 %all-gather.7.cloned.1.call-done = bf16[512,4096]{1,0:T(8,128)(2,1)} async-done(((bf16[64,4096]{1,0:T(8,128)(2,1)}), bf16[512,4096]{1,0:T(8,128)(2,1)}) %all-gather.7.cloned.1.call-update) | async-done | bytes 4194320 | tf_op jit(solution)/shard_map/all_gather | solution.py:45
  107.4 53.3 %all-gather.9.cloned.1.call-done = bf16[4096,640]{1,0:T(8,128)(2,1)} async-done(((bf16[128,640]{1,0:T(8,128)(2,1)}), bf16[4096,640]{1,0:T(8,128)(2,1)}) %all-gather.9.cloned.1.call-update) | async-done | bytes 5242896 | tf_op jit(solution)/shard_map/all_gather | solution.py:47
  160.7 7.4 %fusion.21 = bf16[512,640]{1,0:T(8,128)(2,1)S(1)} fusion(bf16[512,4096]{1,0:T(8,128)(2,1)} %all-gather.7.cloned.1.call-done, bf16[4096,640]{1,0:T(8,128)(2,1)} %all-gather.9.cloned.1.call-done, f32[640]{0:T(1024)S(1)} %convert_element_type.24), kind=kOutput, calls=%fused_computation.26 | convolution fusion | flops 2687631360 | bytes 10095104 | tf_op jit(solution)/shard_map/dot_general | solution.py:23
  168.1 0.3 copy.29
  168.4 2.8 stack.2
  171.2 7.0 %all-to-all-start.2 = ((bf16[8,512,640]{1,2,0:T(8,128)(2,1)}), bf16[8,512,640]{1,2,0:T(8,128)(2,1)}, u32[]{:S(2)}, u32[]{:S(2)}) async-start(bf16[8,512,640]{1,2,0:T(8,128)(2,1)} %stack.2), calls=%async_computation.2 | async-start | bytes 10485760 | tf_op jit(solution)/shard_map/all_to_all | solution.py:52
  178.2 0.5 all-gather.11.cloned.1.call-update
  178.8 34.7 %all-gather.15.cloned.1.call-done = bf16[5120,384]{1,0:T(8,128)(2,1)} async-done(((bf16[160,384]{1,0:T(8,128)(2,1)}), bf16[5120,384]{1,0:T(8,128)(2,1)}) %all-gather.15.cloned.1.call-update) | async-done | bytes 3932176 | tf_op jit(solution)/shard_map/all_gather | solution.py:58
  213.5 84.0 %all-to-all-done.2 = bf16[8,512,640]{1,2,0:T(8,128)(2,1)} async-done(((bf16[8,512,640]{1,2,0:T(8,128)(2,1)}), bf16[8,512,640]{1,2,0:T(8,128)(2,1)}, u32[]{:S(2)}, u32[]{:S(2)}) %all-to-all-start.2) | async-done | bytes 5242912 | tf_op jit(solution)/shard_map/all_to_all | solution.py:52
  297.5 7.4 %convolution_convert_fusion = bf16[512,384]{1,0:T(8,128)(2,1)} fusion(bf16[512,5120]{0,1:T(8,128)(2,1)} %bitcast.2, bf16[5120,384]{1,0:T(8,128)(2,1)} %all-gather.15.cloned.1.call-done), kind=kOutput, calls=%fused_computation.29 | convolution fusion | flops 2013462528 | bytes 9568256 | tf_op jit(solution)/shard_map/dot_general | solution.py:23
  304.9 0.2 all-gather.13.cloned.1.call-start
  305.2 7.5 %fusion.22 = bf16[512,384]{1,0:T(8,128)(2,1)} fusion(bf16[512,5120]{0,1:T(8,128)(2,1)} %bitcast.2, bf16[5120,384]{1,0:T(8,128)(2,1)} %all-gather.11.cloned.1.call-done, f32[384]{0:T(512)S(1)} %convert_element_type.26), kind=kOutput, calls=%fused_computation.28 | convolution fusion | flops 2013659136 | bytes 9569792 | tf_op jit(solution)/shard_map/dot_general | solution.py:23
  312.7 0.3 copy.38
  313.0 0.6 dynamic_slice.3
  313.6 0.6 iota_compare_fusion
  314.3 30.9 %all-gather.17.cloned.1.call-done = bf16[512,3072]{1,0:T(8,128)(2,1)} async-done(((bf16[512,384]{1,0:T(8,128)(2,1)}), bf16[512,3072]{1,0:T(8,128)(2,1)}) %all-gather.17.cloned.1.call-update) | async-done | bytes 3145744 | tf_op jit(solution)/shard_map/all_gather | solution.py:66
  345.1 3.7 fusion.9
  348.8 9.1 %fusion.30 = (f32[24,256]{1,0:T(8,128)S(1)}, f32[24,256,512]{1,2,0:T(8,128)}) fusion(f32[24,512,256]{2,1,0:T(8,128)S(1)} %fusion.9, pred[512]{0:T(512)(128)(4,1)S(1)} %iota_compare_fusion), kind=kOutput, calls=%fused_computation.45 | output fusion | flops 18874880 | bytes 25190912 | tf_op jit(solution)/shard_map/sub | solution.py:16
  357.9 33.0 %all-gather.13.cloned.1.call-done = bf16[512,3072]{1,0:T(8,128)(2,1)} async-done(((bf16[512,384]{1,0:T(8,128)(2,1)}), bf16[512,3072]{1,0:T(8,128)(2,1)}) %all-gather.13.cloned.1.call-update) | async-done | bytes 3145744 | tf_op jit(solution)/shard_map/all_gather | solution.py:67
  390.9 3.2 copy.36
  394.1 6.8 %fusion.12 = bf16[24,128,256]{2,1,0:T(8,128)(2,1)} fusion(bf16[512,24,128]{0,2,1:T(8,128)(2,1)S(1)} %bitcast.39, f32[24,256,512]{1,2,0:T(8,128)} %get-tuple-element.6, f32[24,256]{1,0:T(8,128)S(1)} %get-tuple-element.5), kind=kOutput, calls=%fused_computation.16 | convolution fusion | flops 812384256 | bytes 17326080 | tf_op jit(solution)/shard_map/hrk,khd->rhd/dot_general | solution.py:18
  400.9 2.6 copy.34
  (21 shorter events, 0.3 us)
Async XLA Ops:
  6.5 12.1 %copy-start.3 = (s32[32]{0:T(128)S(1)}, s32[32]{0:T(128)}, u32[]{:S(2)}) copy-start(s32[32]{0:T(128)} %param.10) | copy-start | bytes 388
  8.9 44.2 %copy-start.1 = (bf16[640]{0:T(1024)(128)(2,1)S(1)}, bf16[640]{0:T(1024)(128)(2,1)}, u32[]{:S(2)}) copy-start(bf16[640]{0:T(1024)(128)(2,1)} %param.14) | copy-start | bytes 3844
  10.9 22.1 %all-to-all-start = ((bf16[2,32,2,4096]{3,2,0,1:T(2,128)(2,1)}), bf16[2,32,2,4096]{3,2,0,1:T(2,128)(2,1)S(1)}, u32[]{:S(2)}, u32[]{:S(2)}) async-start(bf16[2,32,2,4096]{3,2,0,1:T(2,128)(2,1)} %copy.28), calls=%async_computation | async-start | bytes 2097152 | tf_op jit(solution)/shard_map/all_to_all | solution.py:32
  18.6 88.8 %all-gather.7.cloned.1.call-start = ((), (), s32[]{:S(2)}) async-start(), calls=%async_computation.3 | async-start | bytes 4718592 | tf_op jit(solution)/shard_map/all_gather | solution.py:45
  51.6 109.1 %all-gather.9.cloned.1.call-start = ((), (), s32[]{:S(2)}) async-start(), calls=%async_computation.4 | async-start | bytes 5406720 | tf_op jit(solution)/shard_map/all_gather | solution.py:47
  52.3 161.2 %all-gather.15.cloned.1.call-start = ((), (), s32[]{:S(2)}) async-start(), calls=%async_computation.7 | async-start | bytes 4055040 | tf_op jit(solution)/shard_map/all_gather | solution.py:58
  171.2 126.4 %all-to-all-start.2 = ((bf16[8,512,640]{1,2,0:T(8,128)(2,1)}), bf16[8,512,640]{1,2,0:T(8,128)(2,1)}, u32[]{:S(2)}, u32[]{:S(2)}) async-start(bf16[8,512,640]{1,2,0:T(8,128)(2,1)} %stack.2), calls=%async_computation.2 | async-start | bytes 10485760 | tf_op jit(solution)/shard_map/all_to_all | solution.py:52
  178.2 127.0 %all-gather.11.cloned.1.call-start = ((), (), s32[]{:S(2)}) async-start(), calls=%async_computation.5 | async-start | bytes 4055040 | tf_op jit(solution)/shard_map/all_gather | solution.py:59
  178.8 166.4 %all-gather.17.cloned.1.call-start = ((), (), s32[]{:S(2)}) async-start(), calls=%async_computation.8 | async-start | bytes 3538944 | tf_op jit(solution)/shard_map/all_gather | solution.py:66
  297.5 7.6 %copy-start.2 = (bf16[384]{0:T(512)(128)(2,1)S(1)}, bf16[384]{0:T(512)(128)(2,1)}, u32[]{:S(2)}) copy-start(bf16[384]{0:T(512)(128)(2,1)} %param.17) | copy-start | bytes 2308
  304.9 86.0 %all-gather.13.cloned.1.call-start = ((), (), s32[]{:S(2)}) async-start(), calls=%async_computation.6 | async-start | bytes 3538944 | tf_op jit(solution)/shard_map/all_gather | solution.py:67
  305.2 7.5 %copy-start = (bf16[1,256,3072]{2,1,0:T(8,128)(2,1)S(1)}, bf16[1,256,3072]{2,1,0:T(8,128)(2,1)}, u32[]{:S(2)}) copy-start(bf16[1,256,3072]{2,1,0:T(8,128)(2,1)} %param.12) | copy-start | bytes 4718596
  305.2 7.9 %copy-start.4 = (s32[32]{0:T(128)S(1)}, s32[32]{0:T(128)}, u32[]{:S(2)}) copy-start(s32[32]{0:T(128)} %param.11) | copy-start | bytes 388
Sparse Core Ops, SparseCore 0:
  51.7 55.6 all-gather.6
  110.0 50.7 all-gather.8
  163.3 50.2 all-gather.14
  215.9 50.2 all-gather.10
  305.0 40.0 all-gather.16
  346.8 44.0 all-gather.12
